TPU v7x, 32 devices: a whole 2x2x4 slice. The times are simulated.
32 devices in a mesh: chan: 8 (over z, y), inp: 4 (over x, core).
Axes of the slice: x: 2, y: 2, z: 4, core: 2. Of those that a mesh axis runs over, the one named last changes fastest.
Arguments:
- voltages: int32 [512, 131072], P('inp', 'chan'), may hold values from -128 to 127
- scales: int32 [512], P('inp'), may hold values from 1 to 5
Outputs:
- visibilities: bfloat16 [2, 1024, 512, 512], P(None, 'chan', 'inp')
All inputs are finite; a program needn't handle non-finite values.
Results may differ from a plain program's by a relative error of at most 0.0069.
Values may be sent and summed in bfloat16 or wider, within the bound.
A program may use at most 192 MiB of HBM per device.

v0:
```python
import math

import jax
import jax.numpy as jnp
from jax import lax
from jax.sharding import PartitionSpec as P

NFFT = 4096
CHANS = 1024
TAPS = 8


def shifted(block, axis, distance):
    devices = range(lax.axis_size(axis))
    route = [(i - distance, i) for i in devices if i - distance in devices]
    return lax.ppermute(block, axis, route)


def window_table():
    count = TAPS * NFFT
    places = jnp.arange(count).astype(jnp.float32)
    shaping = jnp.sinc((places - count / 2.0) / NFFT)
    taper = 0.5 - 0.5 * jnp.cos(2.0 * math.pi * places / count)
    return (shaping * taper).reshape(TAPS, NFFT)


def dft_table():
    columns = jnp.arange(CHANS, dtype=jnp.int32)
    norm_factor = 1.0 / math.sqrt(NFFT)

    def one_block(start):
        rows_idx = start + jnp.arange(512, dtype=jnp.int32)
        phase = rows_idx[:, None] * columns[None, :] % NFFT
        angle = phase.astype(jnp.float32) * (2.0 * math.pi / NFFT)
        return jnp.stack(
            [jnp.cos(angle) * norm_factor, -jnp.sin(angle) * norm_factor], axis=1
        ).astype(jnp.bfloat16)

    starts = jnp.arange(NFFT // 512, dtype=jnp.int32) * 512
    return lax.map(one_block, starts).reshape(NFFT, 2, CHANS)


def filter_taps(padded, window, spec_count):
    total = jnp.zeros((padded.shape[0], spec_count, NFFT), jnp.float32)
    for tap_index in range(TAPS):
        total = total + window[tap_index] * padded[:, tap_index : tap_index + spec_count]
    return total.astype(jnp.bfloat16)


def shards(voltages, scales):
    inp_count = voltages.shape[0]
    shard_len = voltages.shape[1]
    spec_count = shard_len // NFFT
    history_len = (TAPS - 1) * NFFT
    reach_back = -(-history_len // shard_len)
    samples = voltages.astype(jnp.bfloat16)
    earlier = []
    for distance in range(1, reach_back + 1):
        take_count = min(shard_len, history_len - (distance - 1) * shard_len)
        received = shifted(samples[:, shard_len - take_count :], "chan", distance)
        earlier = [received] + earlier
    joined = jnp.concatenate(earlier + [samples], axis=1).astype(jnp.float32)
    signal = joined * scales.astype(jnp.float32)[:, None] * (1.0 / 256.0)
    padded = signal.reshape(inp_count, TAPS - 1 + spec_count, NFFT)
    filtered = filter_taps(padded, window_table(), spec_count)
    spectra = jnp.einsum(
        "isn,nrc->cirs", filtered, dft_table(), preferred_element_type=jnp.float32
    ).astype(jnp.bfloat16)
    local_block = lax.all_to_all(spectra, "chan", split_axis=0, concat_axis=3, tiled=True)
    chan_count = local_block.shape[0]
    spec_total = local_block.shape[3]
    own_rows = local_block.reshape(chan_count, inp_count, 2 * spec_total)
    swapped = jnp.concatenate([own_rows[..., spec_total:], -own_rows[..., :spec_total]], axis=-1)
    piece = lax.all_gather(own_rows, "inp", axis=1, tiled=True)
    real_part = jnp.einsum("cik,cjk->cij", own_rows, piece, preferred_element_type=jnp.float32)
    imag_part = jnp.einsum("cik,cjk->cij", swapped, piece, preferred_element_type=jnp.float32)
    result = jnp.stack([real_part, imag_part]) * (1.0 / spec_total)
    return result.astype(jnp.bfloat16)


def solution(mesh):
    placed = (P("inp", "chan"), P("inp"))
    return jax.shard_map(
        shards, mesh=mesh, in_specs=placed, out_specs=P(None, "chan", "inp", None), check_vma=False
    )
```

profile of v0, /device:TPU:17, one launch (start us, length us, event | category | flops | bytes accessed | tf_op | source)
XLA Modules:
  0.0 428.1 jit_solution(14081009435192580590)
XLA Ops:
  6.5 0.0 all-gather.2.cloned.1.call-start
  6.5 9.0 %copy.16 = s32[128,16384]{0,1:T(8,128)} copy(s32[128,16384]{1,0:T(8,128)} %param.4) | data formatting | bytes 16777216 | tf_op args[0]
  15.5 0.0 copy-start.1
  15.5 5.1 %convert_element_type.91 = bf16[128,16384]{0,1:T(8,128)(2,1)} convert(s32[128,16384]{0,1:T(8,128)} %copy.16) | non-fusion elementwise | flops 2097152 | bytes 12582912 | tf_op jit(solution)/shard_map/convert_element_type | solution.py:56
  20.6 3.1 collective-permute-start.1
  23.8 2.0 slice.85
  25.8 3.2 collective-permute-start
  29.0 0.6 fusion.33
  29.6 0.0 copy-done.1
  29.7 94.0 %while.13 = (s32[]{:T(128)}, bf16[8,512,2,1024]{3,1,0,2:T(8,128)(2,1)}, s32[8]{0:T(128)S(1)}, s32[]{:T(128)}) while((s32[]{:T(128)}, bf16[8,512,2,1024]{3,1,0,2:T(8,128)(2,1)}, s32[8]{0:T(128)S(1)}, s32[]{:T(128)}) %tuple.40), condition=%wide.region_1.2_spmd.clone, body=%wide.region_0.1_spmd.clone.sunk | while | flops 14156290 | bytes 6295633 | solution.py:40
  29.7 0.6 dynamic_slice.9
  30.3 0.6 iota_add_fusion.2
  30.9 9.1 %fusion.51 = (bf16[1,512,1,1024]{3,1,2,0:T(8,128)(2,1)S(1)}, bf16[1,512,1,1024]{3,1,2,0:T(8,128)(2,1)S(1)}) fusion(s32[512]{0:T(512)S(1)} %iota_add_fusion.2), kind=kLoop, calls=%fused_computation.15.clone.1 | loop fusion | flops 9961472 | bytes 2099200 | tf_op jit(solution)/shard_map/while/body/eval_jaxpr/stack | solution.py:35
  40.0 1.6 fusion.52
  41.5 0.6 dynamic_slice.9
  42.1 0.6 iota_add_fusion.2
  42.7 9.1 %fusion.51 = (bf16[1,512,1,1024]{3,1,2,0:T(8,128)(2,1)S(1)}, bf16[1,512,1,1024]{3,1,2,0:T(8,128)(2,1)S(1)}) fusion(s32[512]{0:T(512)S(1)} %iota_add_fusion.2), kind=kLoop, calls=%fused_computation.15.clone.1 | loop fusion | flops 9961472 | bytes 2099200 | tf_op jit(solution)/shard_map/while/body/eval_jaxpr/stack | solution.py:35
  51.8 1.5 fusion.52
  53.2 0.6 dynamic_slice.9
  53.8 0.6 iota_add_fusion.2
  54.4 9.1 %fusion.51 = (bf16[1,512,1,1024]{3,1,2,0:T(8,128)(2,1)S(1)}, bf16[1,512,1,1024]{3,1,2,0:T(8,128)(2,1)S(1)}) fusion(s32[512]{0:T(512)S(1)} %iota_add_fusion.2), kind=kLoop, calls=%fused_computation.15.clone.1 | loop fusion | flops 9961472 | bytes 2099200 | tf_op jit(solution)/shard_map/while/body/eval_jaxpr/stack | solution.py:35
  63.5 1.5 fusion.52
  65.0 0.6 dynamic_slice.9
  65.6 0.6 iota_add_fusion.2
  66.1 9.1 %fusion.51 = (bf16[1,512,1,1024]{3,1,2,0:T(8,128)(2,1)S(1)}, bf16[1,512,1,1024]{3,1,2,0:T(8,128)(2,1)S(1)}) fusion(s32[512]{0:T(512)S(1)} %iota_add_fusion.2), kind=kLoop, calls=%fused_computation.15.clone.1 | loop fusion | flops 9961472 | bytes 2099200 | tf_op jit(solution)/shard_map/while/body/eval_jaxpr/stack | solution.py:35
  75.2 1.5 fusion.52
  76.7 0.6 dynamic_slice.9
  77.3 0.6 iota_add_fusion.2
  77.9 9.1 %fusion.51 = (bf16[1,512,1,1024]{3,1,2,0:T(8,128)(2,1)S(1)}, bf16[1,512,1,1024]{3,1,2,0:T(8,128)(2,1)S(1)}) fusion(s32[512]{0:T(512)S(1)} %iota_add_fusion.2), kind=kLoop, calls=%fused_computation.15.clone.1 | loop fusion | flops 9961472 | bytes 2099200 | tf_op jit(solution)/shard_map/while/body/eval_jaxpr/stack | solution.py:35
  87.0 1.5 fusion.52
  88.5 0.6 dynamic_slice.9
  89.1 0.6 iota_add_fusion.2
  89.7 9.1 %fusion.51 = (bf16[1,512,1,1024]{3,1,2,0:T(8,128)(2,1)S(1)}, bf16[1,512,1,1024]{3,1,2,0:T(8,128)(2,1)S(1)}) fusion(s32[512]{0:T(512)S(1)} %iota_add_fusion.2), kind=kLoop, calls=%fused_computation.15.clone.1 | loop fusion | flops 9961472 | bytes 2099200 | tf_op jit(solution)/shard_map/while/body/eval_jaxpr/stack | solution.py:35
  98.8 1.5 fusion.52
  100.2 0.6 dynamic_slice.9
  100.8 0.6 iota_add_fusion.2
  101.4 9.1 %fusion.51 = (bf16[1,512,1,1024]{3,1,2,0:T(8,128)(2,1)S(1)}, bf16[1,512,1,1024]{3,1,2,0:T(8,128)(2,1)S(1)}) fusion(s32[512]{0:T(512)S(1)} %iota_add_fusion.2), kind=kLoop, calls=%fused_computation.15.clone.1 | loop fusion | flops 9961472 | bytes 2099200 | tf_op jit(solution)/shard_map/while/body/eval_jaxpr/stack | solution.py:35
  110.5 1.5 fusion.52
  112.0 0.6 dynamic_slice.9
  112.5 0.6 iota_add_fusion.2
  113.1 9.1 %fusion.51 = (bf16[1,512,1,1024]{3,1,2,0:T(8,128)(2,1)S(1)}, bf16[1,512,1,1024]{3,1,2,0:T(8,128)(2,1)S(1)}) fusion(s32[512]{0:T(512)S(1)} %iota_add_fusion.2), kind=kLoop, calls=%fused_computation.15.clone.1 | loop fusion | flops 9961472 | bytes 2099200 | tf_op jit(solution)/shard_map/while/body/eval_jaxpr/stack | solution.py:35
  122.2 1.5 fusion.52
  123.7 0.0 collective-permute-done
  123.7 0.0 collective-permute-done.1
  123.7 13.6 %pad_maximum_fusion = bf16[128,45056]{0,1:T(8,128)(2,1)S(1)} fusion(bf16[128,16384]{0,1:T(8,128)(2,1)} %convert_element_type.91, bf16[128,16384]{0,1:T(8,128)(2,1)} %collective-permute-done.1, bf16[128,12288]{0,1:T(8,128)(2,1)} %collective-permute-done), kind=kLoop, calls=%fused_computation.24 | loop fusion | flops 34603008 | bytes 23068672 | tf_op jit(solution)/shard_map/concatenate | solution.py:62
  137.3 8.3 %fusion.12 = f32[128,11,4096]{0,2,1:T(8,128)} fusion(bf16[128,11,4096]{0,2,1:T(8,128)(2,1)S(1)} %bitcast.44, f32[128]{0:T(128)S(1)} %convert_element_type.94), kind=kLoop, calls=%fused_computation.21 | loop fusion | flops 17301504 | bytes 34603520 | tf_op jit(solution)/shard_map/mul | solution.py:63
  145.6 29.6 %convert_bitcast_fusion = bf16[1024,128,2,4]{1,0,3,2:T(8,128)(2,1)S(1)} fusion(bf16[4096,2,1024,1]{2,0,3,1:T(8,128)(2,1)} %bitcast.46, f32[128,11,4096]{0,2,1:T(8,128)} %fusion.12, f32[4096]{0:T(1024)S(1)} %get-tuple-element.79, f32[4096]{0:T(1024)S(1)} %get-tuple-element.80, f32[4096]{0:T(1024)S(1)} %get-tuple-element.81, f32[4096]{0:T(1024)S(1)} %get-tuple-element.82, ...), kind=kOutput, calls=%fused_computation.46 | convolution fusion | flops 8624537600 | bytes 86114304 | tf_op jit(solution)/shard_map/isn,nrc->cirs/dot_general | solution.py:66
  175.3 1.6 copy.19
  176.9 109.1 %all_to_all.15 = bf16[1024,128,2,4]{1,3,2,0:T(4,128)(2,1)S(1)} all-to-all(bf16[1024,128,2,4]{1,3,2,0:T(4,128)(2,1)S(1)} %copy.19), channel_id=1, replica_groups=mesh['chan'=8,'inp'=4] {'chan'}, dimensions={0} | all-to-all | bytes 4194304 | tf_op jit(solution)/shard_map/all_to_all | solution.py:69
  286.0 2.5 copy.20
  288.5 0.0 copy-start
  288.5 0.0 all-gather.2.cloned.1.call-update
  288.6 3.0 fusion.43
  291.5 58.5 %all-gather.2.cloned.1.call-done = bf16[128,512,64]{1,2,0:T(8,128)(2,1)} async-done(((bf16[128,128,64]{1,2,0:T(8,128)(2,1)}), bf16[128,512,64]{1,2,0:T(8,128)(2,1)}) %all-gather.2.cloned.1.call-update) | async-done | bytes 8388624 | tf_op jit(solution)/shard_map/all_gather | solution.py:74
  350.0 0.0 copy-done
  350.0 19.0 %convolution_bitcast_fusion.1 = f32[1,128,128,512]{3,2,1,0:T(8,128)} fusion(bf16[128,128,64]{1,2,0:T(8,128)(2,1)S(1)} %bitcast.43, bf16[128,512,64]{1,2,0:T(8,128)(2,1)} %all-gather.2.cloned.1.call-done), kind=kOutput, calls=%fused_computation.23 | convolution fusion | flops 1073741824 | bytes 44040192 | tf_op jit(solution)/shard_map/cik,cjk->cij/dot_general | solution.py:75
  369.0 19.3 %convolution_bitcast_fusion = f32[1,128,128,512]{3,2,1,0:T(8,128)} fusion(bf16[128,512,64]{1,2,0:T(8,128)(2,1)} %all-gather.2.cloned.1.call-done, bf16[128,128,32]{1,2,0:T(8,128)(2,1)} %get-tuple-element.77, bf16[128,128,32]{1,2,0:T(8,128)(2,1)S(1)} %get-tuple-element.76), kind=kOutput, calls=%fused_computation.22 | convolution fusion | flops 1077936128 | bytes 44040192 | tf_op jit(solution)/shard_map/cik,cjk->cij/dot_general | solution.py:76
  388.4 32.9 %fusion.11 = bf16[2,128,128,512]{3,2,1,0:T(8,128)(2,1)} fusion(f32[1,128,128,512]{3,2,1,0:T(8,128)} %convolution_bitcast_fusion, f32[1,128,128,512]{3,2,1,0:T(8,128)} %convolution_bitcast_fusion.1), kind=kLoop, calls=%fused_computation.19 | loop fusion | flops 50331648 | bytes 100663296 | tf_op jit(solution)/shard_map/convert_element_type | solution.py:78
  (4 shorter events, 0.0 us)
Async XLA Ops:
  6.5 343.5 %all-gather.2.cloned.1.call-start = ((), (), s32[]{:S(2)}) async-start(), calls=%async_computation.1 | async-start | bytes 10485760 | tf_op jit(solution)/shard_map/all_gather | solution.py:74
  15.5 14.1 %copy-start.1 = (s32[128]{0:T(128)S(1)}, s32[128]{0:T(128)}, u32[]{:S(2)}) copy-start(s32[128]{0:T(128)} %param.5) | copy-start | bytes 1540
  20.6 103.1 %collective-permute-start.1 = (bf16[128,16384]{0,1:T(8,128)(2,1)}, bf16[128,16384]{0,1:T(8,128)(2,1)}, u32[]{:S(2)}, u32[]{:S(2)}) collective-permute-start(bf16[128,16384]{0,1:T(8,128)(2,1)} %convert_element_type.91), channel_id=1, source_target_pairs={{0,4},{4,8},{8,12},{12,16},{16,20},{20,24},{24,28},{1,5},{5,9},{9,... | collective-permute-start | bytes 12582920 | tf_op jit(solution)/shard_map/ppermute | solution.py:16
  25.8 97.9 %collective-permute-start = (bf16[128,12288]{0,1:T(8,128)(2,1)S(1)}, bf16[128,12288]{0,1:T(8,128)(2,1)}, u32[]{:S(2)}, u32[]{:S(2)}) collective-permute-start(bf16[128,12288]{0,1:T(8,128)(2,1)S(1)} %slice.85), channel_id=1, source_target_pairs={{0,8},{4,12},{8,16},{12,20},{16,24},{20,28},{1,9},{5,13},{9,17},{1... | collective-permute-start | bytes 9437192 | tf_op jit(solution)/shard_map/ppermute | solution.py:16
  288.5 61.5 %copy-start = (bf16[8,128,128,2,4]{2,4,0,3,1:T(4,128)(2,1)S(1)}, bf16[8,128,128,2,4]{2,4,0,3,1:T(4,128)(2,1)}, u32[]{:S(2)}) copy-start(bf16[8,128,128,2,4]{2,4,0,3,1:T(4,128)(2,1)} %copy.20) | copy-start | bytes 6291460
Sparse Core Ops, SparseCore 0:
  288.7 61.2 all-gather.1
where the time goes:
time: 430 us; the launch traced here: 428 us
  other arithmetic  153 us (36%)
  blocking collectives  109 us (25%)
  matrix products  67.9 us (16%)
  waiting for transfers between devices  58.5 us (14%)
  local copies, waits for them, and re-layouts  19.7 us (5%)
  between operations  13.5 us (3%)
  starting transfers between devices  6.34 us (1%)
    all_to_all x1, blocking collectives, shards(): lax.all_to_all(spectra, 'chan', split_axis=0, concat_axis=3, tiled=True)  109 us
    another operation x8, other arithmetic, one_block(): jnp.stack([jnp.cos(angle) * norm_factor, -jnp.sin(angle) * norm_factor],...  72.7 us
    all_gather x1, waiting for transfers between devices, shards(): piece = lax.all_gather(own_rows, 'inp', axis=1, tiled=True)  58.5 us
    convert_element_type x1, other arithmetic, shards(): return result.astype(jnp.bfloat16)  32.9 us
    dot_general x1, matrix products, shards(): jnp.einsum('isn,nrc->cirs', filtered, dft_table(), preferred_element_type...  29.6 us
    dot_general x1, matrix products, shards(): jnp.einsum('cik,cjk->cij', swapped, piece, preferred_element_type=jnp.flo...  19.3 us
    dot_general x1, matrix products, shards(): jnp.einsum('cik,cjk->cij', own_rows, piece, preferred_element_type=jnp.fl...  19 us
    concatenate x1, other arithmetic, shards(): joined = jnp.concatenate(earlier + [samples], axis=1).astype(jnp.float32)  13.6 us
  transfers between devices with their start and end apart: 3, of which 1 were waited for; matrix products, arithmetic and copies ran while one was open for 23% of the time, Pallas kernels for 0%

commit v1 on v0

--- a/solution.py
+++ b/solution.py
@@ -2,12 +2,17 @@
 
 import jax
 import jax.numpy as jnp
+import ml_dtypes
+import numpy as np
 from jax import lax
+from jax.experimental import pallas as pl
+from jax.experimental.pallas import tpu as pltpu
 from jax.sharding import PartitionSpec as P
 
 NFFT = 4096
 CHANS = 1024
 TAPS = 8
+MESH = pl.DeviceIdType.MESH
 
 
 def shifted(block, axis, distance):
@@ -78,8 +83,197 @@
     return result.astype(jnp.bfloat16)
 
 
+SUBS = 4
+PART = 11
+
+
+def fold_tables():
+    places = np.arange(TAPS * NFFT).astype(np.float64)
+    window = np.sinc((places - TAPS * NFFT / 2) / NFFT) * (0.5 - 0.5 * np.cos(2 * np.pi * places / (TAPS * NFFT)))
+    window = window.reshape(TAPS, NFFT).astype(np.float32)
+    edge = np.zeros((4, NFFT), np.float32)
+    wide = np.concatenate([edge, window, edge], axis=0)
+    m = np.arange(NFFT // 4)
+    out = []
+    for e in range(4):
+        c = 4 * np.arange(CHANS // 4) + e
+        angle = 2 * np.pi * ((m[None, :] * c[:, None]) % NFFT) / NFFT
+        co, si = np.cos(angle) / 64, np.sin(angle) / 64
+        if e % 2 == 0:
+            re, im = co, -si
+        elif e == 1:
+            re, im = np.concatenate([co, -si], 1), np.concatenate([-si, -co], 1)
+        else:
+            re, im = np.concatenate([co, si], 1), np.concatenate([-si, co], 1)
+        groups = 8
+        both = np.stack([re.reshape(groups, -1, re.shape[1]), im.reshape(groups, -1, re.shape[1])], axis=1)
+        out.append(both.reshape(-1, re.shape[1]).astype(ml_dtypes.bfloat16))
+    return wide, np.stack([out[0], out[2]]), np.stack([out[1], out[3]])
+
+
+def front_kernel(x_ref, g_ref, w_ref, even_ref, odd_ref, o_ref, y_ref):
+    p = pl.program_id(0)
+    rows, span, quarter = 32, 256, NFFT // 4
+
+    for half in range(2):
+        s = 2 * p + half
+
+        @pl.loop(0, 128 // rows)
+        def _(i):
+            r0 = pl.multiple_of(i * rows, rows)
+            gain = g_ref[pl.ds(r0, rows), :]
+            for l in range(quarter // span):
+                f = []
+                for q in range(4):
+                    acc = None
+                    for b in range(4):
+                        col = q * quarter + l * span
+                        x = x_ref[pl.ds(r0, rows), b * NFFT + col:b * NFFT + col + span].astype(jnp.float32)
+                        term = x * w_ref[b + 11 - s, :, col:col + span]
+                        acc = term if acc is None else acc + term
+                    f.append(acc)
+                a, b2 = f[0] + f[2], f[1] + f[3]
+                at = pl.ds(half * 128 + r0, rows)
+                for j, v in enumerate((a + b2, a - b2, f[0] - f[2], f[1] - f[3])):
+                    y_ref[at, j * quarter + l * span:j * quarter + (l + 1) * span] = (v * gain).astype(jnp.bfloat16)
+
+    nt = (((1,), (1,)), ((), ()))
+    for e in range(4):
+        for part in range(2):
+            sel = pl.ds(part * 256, 256)
+            if e % 2 == 0:
+                tab, y = even_ref[e // 2, sel, :], y_ref[:, (e // 2) * quarter:(e // 2 + 1) * quarter]
+            else:
+                tab, y = odd_ref[e // 2, sel, :], y_ref[:, 2 * quarter:]
+            res = lax.dot_general(tab, y, nt, preferred_element_type=jnp.float32).astype(jnp.bfloat16)
+            for half in range(2):
+                o_ref[4 * part:4 * part + 4, e, half] = res[:, half * 128:(half + 1) * 128].reshape(4, 2, 32, 128)
+
+
+def comm_kernel(p_ref, o_ref, got, own, send_sem, recv_sem, loc_sem, xsend, xrecv):
+    me = lax.axis_index("chan")
+    inp = lax.axis_index("inp")
+    mate = inp + 1 - 2 * lax.rem(inp, 2)
+    across = lax.rem(inp + 2, 4)
+    barrier = pltpu.get_barrier_semaphore()
+    for k in range(1, 8):
+        pl.semaphore_signal(barrier, inc=1, device_id={"chan": lax.rem(me + k, 8)}, device_id_type=MESH)
+    for other in (mate, across):
+        pl.semaphore_signal(barrier, inc=1, device_id={"inp": other}, device_id_type=MESH)
+    pl.semaphore_wait(barrier, 9)
+
+    def turn(e, k):
+        return pltpu.make_async_remote_copy(
+            src_ref=p_ref.at[lax.rem(me + k, 8), e, pl.ds(0, PART)], dst_ref=got.at[me, e],
+            send_sem=send_sem.at[e, k], recv_sem=recv_sem.at[e, k],
+            device_id={"chan": lax.rem(me + k, 8)}, device_id_type=MESH)
+
+    def stay(e):
+        return pltpu.make_async_copy(p_ref.at[me, e, pl.ds(0, PART)], got.at[me, e], recv_sem.at[e, 0])
+
+    def pair(e, which):
+        src = own.at[e] if which < 2 else o_ref.at[across, e]
+        dst = o_ref.at[inp, e] if which < 2 else o_ref.at[across, e]
+        return pltpu.make_async_remote_copy(
+            src_ref=src, dst_ref=dst, send_sem=xsend.at[e, which], recv_sem=xrecv.at[e, which],
+            device_id={"inp": across if which == 0 else mate}, device_id_type=MESH)
+
+    def keep(e):
+        return pltpu.make_async_copy(own.at[e], o_ref.at[inp, e], loc_sem.at[e])
+
+    for e in range(SUBS):
+        for k in range(1, 8):
+            turn(e, k).start()
+        stay(e).start()
+    for e in range(SUBS):
+        stay(e).wait()
+        for k in range(1, 8):
+            turn(e, k).wait_recv()
+        for s in range(32):
+            total = None
+            for src in range(max(0, s // 4 - 2), s // 4 + 1):
+                if s - 4 * src < PART:
+                    term = got[src, e, s - 4 * src].astype(jnp.float32)
+                    total = term if total is None else total + term
+            own[e, s] = total.astype(jnp.bfloat16)
+        pair(e, 0).start()
+        pair(e, 1).start()
+        keep(e).start()
+        if e:
+            pair(e - 1, 0).wait_recv()
+            pair(e - 1, 2).start()
+    pair(SUBS - 1, 0).wait_recv()
+    pair(SUBS - 1, 2).start()
+    for e in range(SUBS):
+        for k in range(1, 8):
+            turn(e, k).wait_send()
+        keep(e).wait()
+        pair(e, 0).wait_send()
+        pair(e, 1).wait()
+        pair(e, 2).wait()
+
+
+def pair_kernel(me_ref, all_ref, own_ref, o_ref):
+    del me_ref
+    for e in range(4):
+        for d in range(2):
+            own = own_ref[e, d]
+            both = jnp.concatenate([jnp.concatenate([own[:32], own[32:]], axis=0),
+                                    jnp.concatenate([own[32:], -own[:32]], axis=0)], axis=1)
+            res = lax.dot_general(both, all_ref[e, d], (((0,), (0,)), ((), ())), preferred_element_type=jnp.float32)
+            res = (res * (1.0 / 32.0)).astype(jnp.bfloat16)
+            o_ref[0, 4 * d + e] = res[:128]
+            o_ref[1, 4 * d + e] = res[128:]
+
+
+def fast(voltages, scales):
+    wide, even, odd = (jnp.asarray(t) for t in fold_tables())
+    gains = (scales.astype(jnp.float32) * (1.0 / 256.0))[:, None]
+    whole = lambda *shape: pl.BlockSpec(shape, lambda p: (0,) * len(shape))
+    parts = pl.pallas_call(
+        front_kernel, grid=(6,),
+        out_shape=jax.ShapeDtypeStruct((8, 4, 12, 2, 32, 128), jnp.bfloat16),
+        in_specs=[whole(128, 16384), whole(128, 1), whole(16, 1, NFFT), whole(2, 512, 1024), whole(2, 512, 2048)],
+        out_specs=pl.BlockSpec((8, 4, 2, 2, 32, 128), lambda p: (0, 0, p, 0, 0, 0)),
+        scratch_shapes=[pltpu.VMEM((256, NFFT), jnp.bfloat16)],
+        compiler_params=pltpu.CompilerParams(vmem_limit_bytes=56 << 20),
+        name="filter_transform",
+    )(voltages, gains, wide[:, None], even, odd)
+    gathered = pl.pallas_call(
+        comm_kernel,
+        out_shape=jax.ShapeDtypeStruct((4, 4, 32, 2, 32, 128), jnp.bfloat16),
+        in_specs=[pl.BlockSpec(memory_space=pl.ANY)],
+        out_specs=pl.BlockSpec(memory_space=pl.ANY),
+        scratch_shapes=[
+            pltpu.VMEM((8, SUBS, PART, 2, 32, 128), jnp.bfloat16),
+            pltpu.VMEM((SUBS, 32, 2, 32, 128), jnp.bfloat16),
+            pltpu.SemaphoreType.DMA((SUBS, 8)), pltpu.SemaphoreType.DMA((SUBS, 8)),
+            pltpu.SemaphoreType.DMA((SUBS,)),
+            pltpu.SemaphoreType.DMA((SUBS, 3)), pltpu.SemaphoreType.DMA((SUBS, 3)),
+        ],
+        compiler_params=pltpu.CompilerParams(
+            collective_id=0, has_side_effects=True, vmem_limit_bytes=48 << 20),
+        name="turn_and_share",
+    )(parts)
+    lined = gathered.transpose(1, 4, 3, 2, 0, 5).reshape(4, 32, 64, 512)
+    me = lax.axis_index("inp").astype(jnp.int32).reshape(1)
+    return pl.pallas_call(
+        pair_kernel,
+        out_shape=jax.ShapeDtypeStruct((2, 128, 128, 512), jnp.bfloat16),
+        grid_spec=pltpu.PrefetchScalarGridSpec(
+            num_scalar_prefetch=1, grid=(16,),
+            in_specs=[pl.BlockSpec((4, 2, 64, 512), lambda g, m: (0, g, 0, 0)),
+                      pl.BlockSpec((4, 2, 64, 128), lambda g, m: (0, g, 0, m[0]))],
+            out_specs=pl.BlockSpec((2, 8, 128, 512), lambda g, m: (0, g, 0, 0))),
+        compiler_params=pltpu.CompilerParams(vmem_limit_bytes=48 << 20),
+        name="correlate",
+    )(me, lined, lined)
+
+
 def solution(mesh):
     placed = (P("inp", "chan"), P("inp"))
+    sizes = (mesh.shape["chan"], mesh.shape["inp"])
     return jax.shard_map(
-        shards, mesh=mesh, in_specs=placed, out_specs=P(None, "chan", "inp", None), check_vma=False
+        fast if sizes == (8, 4) else shards,
+        mesh=mesh, in_specs=placed, out_specs=P(None, "chan", "inp", None), check_vma=False
     )

time: 430 us -> 224 us (0.52)
  the two profiles are of different devices: /device:TPU:17 before, /device:TPU:13 now
where the time goes in v1:
time: 224 us; the launch traced here: 223 us
  Pallas kernels  196 us (88%)
  local copies, waits for them, and re-layouts  26 us (12%)
    pallas_call x1, Pallas kernels, fast(): pl.pallas_call(comm_kernel, out_shape=jax.ShapeDtypeStruct((4, 4, 32, 2,...  145 us
    pallas_call x1, Pallas kernels, fast(): pl.pallas_call(front_kernel, grid=(6,), out_shape=jax.ShapeDtypeStruct((8...  29.6 us
    pallas_call x1, Pallas kernels, fast(): pl.pallas_call(pair_kernel, out_shape=jax.ShapeDtypeStruct((2, 128, 128,...  21.2 us
    reshape x1, local copies, waits for them, and re-layouts, fast(): lined = gathered.transpose(1, 4, 3, 2, 0, 5).reshape(4, 32, 64, 512)  13.1 us
    transpose x1, local copies, waits for them, and re-layouts, fast(): lined = gathered.transpose(1, 4, 3, 2, 0, 5).reshape(4, 32, 64, 512)  12.2 us

profile of v1, /device:TPU:13, one launch (start us, length us, event | category | flops | bytes accessed | tf_op | source)
XLA Modules:
  0.0 223.0 jit_solution(11735301379140431386)
XLA Ops:
  0.0 0.7 multiply_bitcast_fusion
  0.7 0.7 copy.6.g_ref
  1.4 29.6 %filter_transform.1.p_ref = bf16[8,4,12,2,32,128]{5,4,3,2,1,0:T(8,128)(2,1)} custom-call(s32[128,16384]{1,0:T(8,128)} %x_ref.1, f32[128,1]{1,0:T(8,128)} %copy.6.g_ref, f32[16,1,4096]{2,1,0:T(1,128)} %constant.15.w_ref, bf16[2,512,1024]{2,1,0:T(8,128)(2,1)} %constant.13.clone.even_ref, bf16[2,512,2048]{2,1,0:T(8,128)(2,1)} %constant.14.clone.odd_ref), custom_call_target="tpu_custom_call" | custom-call | tf_op jit(solution)/shard_map/filter_transform/pallas_call | solution.py:233
  31.0 145.5 %turn_and_share.1 = bf16[4,4,32,2,32,128]{5,4,3,2,1,0:T(8,128)(2,1)} custom-call(bf16[8,4,12,2,32,128]{5,4,3,2,1,0:T(8,128)(2,1)} %filter_transform.1.p_ref), custom_call_target="tpu_custom_call" | custom-call | tf_op jit(solution)/shard_map/turn_and_share/pallas_call | solution.py:242
  176.5 12.2 %copy.7 = bf16[4,32,2,32,4,128]{5,4,3,2,1,0:T(4,128)(2,1)} copy(bf16[4,32,2,32,4,128]{5,1,2,3,0,4:T(8,128)(2,1)} %bitcast.4) | data formatting | bytes 16777216 | tf_op jit(solution)/shard_map/transpose | solution.py:258
  188.7 13.1 %reshape.7.all_ref.own_ref = bf16[4,32,64,512]{3,2,1,0:T(8,128)(2,1)} reshape(bf16[4,32,2,32,4,128]{5,4,3,2,1,0:T(4,128)(2,1)} %copy.7) | data formatting | bytes 16777216 | tf_op jit(solution)/shard_map/reshape | solution.py:258
  201.8 21.2 %correlate.1 = bf16[2,128,128,512]{3,2,1,0:T(8,128)(2,1)} custom-call(s32[1]{0:T(128)} %bitcast.me_ref, bf16[4,32,64,512]{3,2,1,0:T(8,128)(2,1)} %reshape.7.all_ref.own_ref, bf16[4,32,64,512]{3,2,1,0:T(8,128)(2,1)} %reshape.7.all_ref.own_ref), custom_call_target="tpu_custom_call" | custom-call | tf_op jit(solution)/shard_map/correlate/pallas_call | solution.py:260

commit v2 on v1

--- a/solution.py
+++ b/solution.py
@@ -147,29 +147,46 @@
                 tab, y = odd_ref[e // 2, sel, :], y_ref[:, 2 * quarter:]
             res = lax.dot_general(tab, y, nt, preferred_element_type=jnp.float32).astype(jnp.bfloat16)
             for half in range(2):
-                o_ref[4 * part:4 * part + 4, e, half] = res[:, half * 128:(half + 1) * 128].reshape(4, 2, 32, 128)
-
-
-def comm_kernel(p_ref, o_ref, got, own, send_sem, recv_sem, loc_sem, xsend, xrecv):
+                blocks = res[:, half * 128:(half + 1) * 128].reshape(2, 2, 2, 32, 128)
+                for y in range(2):
+                    o_ref[y, e, 2 * part:2 * part + 2, half] = blocks[:, y]
+
+
+def comm_kernel(p_ref, o_ref, near, comb, got, own, ysend, yrecv, zsend, zrecv, loc_sem, xsend, xrecv):
     me = lax.axis_index("chan")
     inp = lax.axis_index("inp")
+    z, y = me // 2, lax.rem(me, 2)
+    twin = 2 * z + 1 - y
     mate = inp + 1 - 2 * lax.rem(inp, 2)
     across = lax.rem(inp + 2, 4)
+
+    def far(k):
+        return lax.rem(z + k, 4)
+
     barrier = pltpu.get_barrier_semaphore()
-    for k in range(1, 8):
-        pl.semaphore_signal(barrier, inc=1, device_id={"chan": lax.rem(me + k, 8)}, device_id_type=MESH)
+    for other in (twin, 2 * far(1) + y, 2 * far(2) + y, 2 * far(3) + y):
+        pl.semaphore_signal(barrier, inc=1, device_id={"chan": other}, device_id_type=MESH)
     for other in (mate, across):
         pl.semaphore_signal(barrier, inc=1, device_id={"inp": other}, device_id_type=MESH)
-    pl.semaphore_wait(barrier, 9)
+    pl.semaphore_wait(barrier, 6)
+
+    def first(e):
+        return pltpu.make_async_remote_copy(
+            src_ref=p_ref.at[1 - y, e, :, pl.ds(0, PART)], dst_ref=near.at[y, e],
+            send_sem=ysend.at[e], recv_sem=yrecv.at[e],
+            device_id={"chan": twin}, device_id_type=MESH)
+
+    def mine(e):
+        return pltpu.make_async_copy(p_ref.at[y, e, :, pl.ds(0, PART)], near.at[y, e], loc_sem.at[e, 0])
 
     def turn(e, k):
         return pltpu.make_async_remote_copy(
-            src_ref=p_ref.at[lax.rem(me + k, 8), e, pl.ds(0, PART)], dst_ref=got.at[me, e],
-            send_sem=send_sem.at[e, k], recv_sem=recv_sem.at[e, k],
-            device_id={"chan": lax.rem(me + k, 8)}, device_id_type=MESH)
+            src_ref=comb.at[e, far(k)], dst_ref=got.at[z, e],
+            send_sem=zsend.at[e, k], recv_sem=zrecv.at[e, k],
+            device_id={"chan": 2 * far(k) + y}, device_id_type=MESH)
 
     def stay(e):
-        return pltpu.make_async_copy(p_ref.at[me, e, pl.ds(0, PART)], got.at[me, e], recv_sem.at[e, 0])
+        return pltpu.make_async_copy(comb.at[e, z], got.at[z, e], loc_sem.at[e, 1])
 
     def pair(e, which):
         src = own.at[e] if which < 2 else o_ref.at[across, e]
@@ -179,33 +196,67 @@
             device_id={"inp": across if which == 0 else mate}, device_id_type=MESH)
 
     def keep(e):
-        return pltpu.make_async_copy(own.at[e], o_ref.at[inp, e], loc_sem.at[e])
-
-    for e in range(SUBS):
-        for k in range(1, 8):
+        return pltpu.make_async_copy(own.at[e], o_ref.at[inp, e], loc_sem.at[e, 2])
+
+    def join_twins(e):
+        mine(e).wait()
+        first(e).wait_recv()
+
+        @pl.loop(0, 4)
+        def _(to):
+            for j in range(PART + 4):
+                total = None
+                for src in range(2):
+                    if 0 <= j - 4 * src < PART:
+                        term = near[src, e, to, j - 4 * src].astype(jnp.float32)
+                        total = term if total is None else total + term
+                comb[e, to, j] = total.astype(jnp.bfloat16)
+
+        for k in (2, 1, 3):
             turn(e, k).start()
         stay(e).start()
-    for e in range(SUBS):
+
+    def join_all(e):
         stay(e).wait()
-        for k in range(1, 8):
+        for k in range(1, 4):
             turn(e, k).wait_recv()
-        for s in range(32):
-            total = None
-            for src in range(max(0, s // 4 - 2), s // 4 + 1):
-                if s - 4 * src < PART:
-                    term = got[src, e, s - 4 * src].astype(jnp.float32)
-                    total = term if total is None else total + term
-            own[e, s] = total.astype(jnp.bfloat16)
+
+        @pl.loop(0, 4)
+        def _(i):
+            r, d0 = i // 2, pl.multiple_of(lax.rem(i, 2) * 16, 16)
+            rows = []
+            for s in range(32):
+                src, j = s // 8, s % 8
+                total = got[src, e, j, r, pl.ds(d0, 16), :].astype(jnp.float32)
+                if src and j < 7:
+                    total = total + got[src - 1, e, j + 8, r, pl.ds(d0, 16), :].astype(jnp.float32)
+                rows.append(total)
+            lined = jnp.swapaxes(jnp.stack(rows), 0, 1)
+            own[e, pl.ds(d0, 16), pl.ds(pl.multiple_of(r * 32, 32), 32), :] = lined.astype(jnp.bfloat16)
+
         pair(e, 0).start()
         pair(e, 1).start()
         keep(e).start()
         if e:
             pair(e - 1, 0).wait_recv()
             pair(e - 1, 2).start()
+
+    for e in range(SUBS):
+        first(e).start()
+        mine(e).start()
+    join_twins(0)
+    join_twins(1)
+    join_all(0)
+    join_twins(2)
+    join_all(1)
+    join_twins(3)
+    join_all(2)
+    join_all(3)
     pair(SUBS - 1, 0).wait_recv()
     pair(SUBS - 1, 2).start()
     for e in range(SUBS):
-        for k in range(1, 8):
+        first(e).wait_send()
+        for k in range(1, 4):
             turn(e, k).wait_send()
         keep(e).wait()
         pair(e, 0).wait_send()
@@ -217,10 +268,11 @@
     del me_ref
     for e in range(4):
         for d in range(2):
-            own = own_ref[e, d]
+            own = own_ref[0, e, d]
             both = jnp.concatenate([jnp.concatenate([own[:32], own[32:]], axis=0),
                                     jnp.concatenate([own[32:], -own[:32]], axis=0)], axis=1)
-            res = lax.dot_general(both, all_ref[e, d], (((0,), (0,)), ((), ())), preferred_element_type=jnp.float32)
+            every = jnp.concatenate([all_ref[i, e, d] for i in range(4)], axis=1)
+            res = lax.dot_general(both, every, (((0,), (0,)), ((), ())), preferred_element_type=jnp.float32)
             res = (res * (1.0 / 32.0)).astype(jnp.bfloat16)
             o_ref[0, 4 * d + e] = res[:128]
             o_ref[1, 4 * d + e] = res[128:]
@@ -232,42 +284,44 @@
     whole = lambda *shape: pl.BlockSpec(shape, lambda p: (0,) * len(shape))
     parts = pl.pallas_call(
         front_kernel, grid=(6,),
-        out_shape=jax.ShapeDtypeStruct((8, 4, 12, 2, 32, 128), jnp.bfloat16),
+        out_shape=jax.ShapeDtypeStruct((2, 4, 4, 12, 2, 32, 128), jnp.bfloat16),
         in_specs=[whole(128, 16384), whole(128, 1), whole(16, 1, NFFT), whole(2, 512, 1024), whole(2, 512, 2048)],
-        out_specs=pl.BlockSpec((8, 4, 2, 2, 32, 128), lambda p: (0, 0, p, 0, 0, 0)),
+        out_specs=pl.BlockSpec((2, 4, 4, 2, 2, 32, 128), lambda p: (0, 0, 0, p, 0, 0, 0)),
         scratch_shapes=[pltpu.VMEM((256, NFFT), jnp.bfloat16)],
         compiler_params=pltpu.CompilerParams(vmem_limit_bytes=56 << 20),
         name="filter_transform",
     )(voltages, gains, wide[:, None], even, odd)
     gathered = pl.pallas_call(
         comm_kernel,
-        out_shape=jax.ShapeDtypeStruct((4, 4, 32, 2, 32, 128), jnp.bfloat16),
+        out_shape=jax.ShapeDtypeStruct((4, SUBS, 32, 64, 128), jnp.bfloat16),
         in_specs=[pl.BlockSpec(memory_space=pl.ANY)],
         out_specs=pl.BlockSpec(memory_space=pl.ANY),
         scratch_shapes=[
-            pltpu.VMEM((8, SUBS, PART, 2, 32, 128), jnp.bfloat16),
-            pltpu.VMEM((SUBS, 32, 2, 32, 128), jnp.bfloat16),
-            pltpu.SemaphoreType.DMA((SUBS, 8)), pltpu.SemaphoreType.DMA((SUBS, 8)),
-            pltpu.SemaphoreType.DMA((SUBS,)),
+            pltpu.VMEM((2, SUBS, 4, PART, 2, 32, 128), jnp.bfloat16),
+            pltpu.VMEM((SUBS, 4, PART + 4, 2, 32, 128), jnp.bfloat16),
+            pltpu.VMEM((4, SUBS, PART + 4, 2, 32, 128), jnp.bfloat16),
+            pltpu.VMEM((SUBS, 32, 64, 128), jnp.bfloat16),
+            pltpu.SemaphoreType.DMA((SUBS,)), pltpu.SemaphoreType.DMA((SUBS,)),
+            pltpu.SemaphoreType.DMA((SUBS, 4)), pltpu.SemaphoreType.DMA((SUBS, 4)),
+            pltpu.SemaphoreType.DMA((SUBS, 3)),
             pltpu.SemaphoreType.DMA((SUBS, 3)), pltpu.SemaphoreType.DMA((SUBS, 3)),
         ],
         compiler_params=pltpu.CompilerParams(
             collective_id=0, has_side_effects=True, vmem_limit_bytes=48 << 20),
         name="turn_and_share",
     )(parts)
-    lined = gathered.transpose(1, 4, 3, 2, 0, 5).reshape(4, 32, 64, 512)
     me = lax.axis_index("inp").astype(jnp.int32).reshape(1)
     return pl.pallas_call(
         pair_kernel,
         out_shape=jax.ShapeDtypeStruct((2, 128, 128, 512), jnp.bfloat16),
         grid_spec=pltpu.PrefetchScalarGridSpec(
             num_scalar_prefetch=1, grid=(16,),
-            in_specs=[pl.BlockSpec((4, 2, 64, 512), lambda g, m: (0, g, 0, 0)),
-                      pl.BlockSpec((4, 2, 64, 128), lambda g, m: (0, g, 0, m[0]))],
+            in_specs=[pl.BlockSpec((4, 4, 2, 64, 128), lambda g, m: (0, 0, g, 0, 0)),
+                      pl.BlockSpec((1, 4, 2, 64, 128), lambda g, m: (m[0], 0, g, 0, 0))],
             out_specs=pl.BlockSpec((2, 8, 128, 512), lambda g, m: (0, g, 0, 0))),
         compiler_params=pltpu.CompilerParams(vmem_limit_bytes=48 << 20),
         name="correlate",
-    )(me, lined, lined)
+    )(me, gathered, gathered)
 
 
 def solution(mesh):

time: 224 us -> 175 us (0.78)
  the two profiles are of different devices: /device:TPU:13 before, /device:TPU:17 now
where the time goes in v2:
time: 175 us; the launch traced here: 174 us
  Pallas kernels  173 us (99%)
    pallas_call x1, Pallas kernels, fast(): pl.pallas_call(comm_kernel, out_shape=jax.ShapeDtypeStruct((4, SUBS, 32,...  122 us
    pallas_call x1, Pallas kernels, fast(): pl.pallas_call(front_kernel, grid=(6,), out_shape=jax.ShapeDtypeStruct((2...  29.6 us
    pallas_call x1, Pallas kernels, fast(): pl.pallas_call(pair_kernel, out_shape=jax.ShapeDtypeStruct((2, 128, 128,...  21.1 us

profile of v2, /device:TPU:17, one launch (start us, length us, event | category | flops | bytes accessed | tf_op | source)
XLA Modules:
  0.0 174.0 jit_solution(5737950722113969670)
XLA Ops:
  0.0 0.7 multiply_bitcast_fusion
  0.7 0.7 copy.6.g_ref
  1.4 29.6 %filter_transform.1.p_ref = bf16[2,4,4,12,2,32,128]{6,5,4,3,2,1,0:T(8,128)(2,1)} custom-call(s32[128,16384]{1,0:T(8,128)} %x_ref.1, f32[128,1]{1,0:T(8,128)} %copy.6.g_ref, f32[16,1,4096]{2,1,0:T(1,128)} %constant.15.w_ref, bf16[2,512,1024]{2,1,0:T(8,128)(2,1)} %constant.13.clone.even_ref, bf16[2,512,2048]{2,1,0:T(8,128)(2,1)} %constant.14.clone.odd_ref), custom_call_target="tpu_custom_call" | custom-call | tf_op jit(solution)/shard_map/filter_transform/pallas_call | solution.py:285
  31.0 121.8 %turn_and_share.1.all_ref.own_ref = bf16[4,4,32,64,128]{4,3,2,1,0:T(8,128)(2,1)} custom-call(bf16[2,4,4,12,2,32,128]{6,5,4,3,2,1,0:T(8,128)(2,1)} %filter_transform.1.p_ref), custom_call_target="tpu_custom_call" | custom-call | tf_op jit(solution)/shard_map/turn_and_share/pallas_call | solution.py:294
  152.9 21.1 %correlate.1 = bf16[2,128,128,512]{3,2,1,0:T(8,128)(2,1)} custom-call(s32[1]{0:T(128)} %bitcast.me_ref, bf16[4,4,32,64,128]{4,3,2,1,0:T(8,128)(2,1)} %turn_and_share.1.all_ref.own_ref, bf16[4,4,32,64,128]{4,3,2,1,0:T(8,128)(2,1)} %turn_and_share.1.all_ref.own_ref), custom_call_target="tpu_custom_call" | custom-call | tf_op jit(solution)/shard_map/correlate/pallas_call | solution.py:314

commit v3 on v2

--- a/solution.py
+++ b/solution.py
@@ -83,7 +83,7 @@
     return result.astype(jnp.bfloat16)
 
 
-SUBS = 4
+SUBS = 8
 PART = 11
 
 
@@ -91,8 +91,7 @@
     places = np.arange(TAPS * NFFT).astype(np.float64)
     window = np.sinc((places - TAPS * NFFT / 2) / NFFT) * (0.5 - 0.5 * np.cos(2 * np.pi * places / (TAPS * NFFT)))
     window = window.reshape(TAPS, NFFT).astype(np.float32)
-    edge = np.zeros((4, NFFT), np.float32)
-    wide = np.concatenate([edge, window, edge], axis=0)
+    wide = np.concatenate([np.zeros((6, NFFT), np.float32), window, np.zeros((4, NFFT), np.float32)], axis=0)
     m = np.arange(NFFT // 4)
     out = []
     for e in range(4):
@@ -111,34 +110,37 @@
     return wide, np.stack([out[0], out[2]]), np.stack([out[1], out[3]])
 
 
-def front_kernel(x_ref, g_ref, w_ref, even_ref, odd_ref, o_ref, y_ref):
+def front_kernel(x_ref, g_ref, w_ref, even_ref, odd_ref, o_ref, f_ref, new_ref, y_ref):
     p = pl.program_id(0)
     rows, span, quarter = 32, 256, NFFT // 4
-
-    for half in range(2):
+    nt = (((1,), (1,)), ((), ()))
+
+    @pl.when(p == 0)
+    def _():
+        @pl.loop(0, 32)
+        def _(i):
+            cols = pl.ds(pl.multiple_of(i * 512, 512), 512)
+            f_ref[:, cols] = x_ref[:, cols].astype(jnp.float32) * g_ref[...]
+
+    def filter_rows(half, r0):
         s = 2 * p + half
-
-        @pl.loop(0, 128 // rows)
-        def _(i):
-            r0 = pl.multiple_of(i * rows, rows)
-            gain = g_ref[pl.ds(r0, rows), :]
-            for l in range(quarter // span):
-                f = []
-                for q in range(4):
-                    acc = None
-                    for b in range(4):
-                        col = q * quarter + l * span
-                        x = x_ref[pl.ds(r0, rows), b * NFFT + col:b * NFFT + col + span].astype(jnp.float32)
-                        term = x * w_ref[b + 11 - s, :, col:col + span]
-                        acc = term if acc is None else acc + term
-                    f.append(acc)
-                a, b2 = f[0] + f[2], f[1] + f[3]
-                at = pl.ds(half * 128 + r0, rows)
-                for j, v in enumerate((a + b2, a - b2, f[0] - f[2], f[1] - f[3])):
-                    y_ref[at, j * quarter + l * span:j * quarter + (l + 1) * span] = (v * gain).astype(jnp.bfloat16)
-
-    nt = (((1,), (1,)), ((), ()))
+        for l in range(quarter // span):
+            f = []
+            for q in range(4):
+                acc = None
+                col = q * quarter + l * span
+                for b in range(4):
+                    term = f_ref[r0:r0 + rows, b * NFFT + col:b * NFFT + col + span] * w_ref[b + 13 - s, :, col:col + span]
+                    acc = term if acc is None else acc + term
+                f.append(acc)
+            a, b2 = f[0] + f[2], f[1] + f[3]
+            at = half * 128 + r0
+            for j, v in enumerate((a + b2, a - b2, f[0] - f[2], f[1] - f[3])):
+                new_ref[at:at + rows, j * quarter + l * span:j * quarter + (l + 1) * span] = v.astype(jnp.bfloat16)
+
     for e in range(4):
+        filter_rows(0, e * rows)
+        filter_rows(1, e * rows)
         for part in range(2):
             sel = pl.ds(part * 256, 256)
             if e % 2 == 0:
@@ -147,9 +149,11 @@
                 tab, y = odd_ref[e // 2, sel, :], y_ref[:, 2 * quarter:]
             res = lax.dot_general(tab, y, nt, preferred_element_type=jnp.float32).astype(jnp.bfloat16)
             for half in range(2):
-                blocks = res[:, half * 128:(half + 1) * 128].reshape(2, 2, 2, 32, 128)
-                for y in range(2):
-                    o_ref[y, e, 2 * part:2 * part + 2, half] = blocks[:, y]
+                blocks = res[:, half * 128:(half + 1) * 128].reshape(2, 2, 2, 2, 16, 128)
+                for y_to in range(2):
+                    for d in range(2):
+                        o_ref[y_to, 2 * e + d, 2 * part:2 * part + 2, half] = blocks[:, y_to, :, d]
+    y_ref[...] = new_ref[...]
 
 
 def comm_kernel(p_ref, o_ref, near, comb, got, own, ysend, yrecv, zsend, zrecv, loc_sem, xsend, xrecv):
@@ -221,18 +225,17 @@
         for k in range(1, 4):
             turn(e, k).wait_recv()
 
-        @pl.loop(0, 4)
-        def _(i):
-            r, d0 = i // 2, pl.multiple_of(lax.rem(i, 2) * 16, 16)
+        @pl.loop(0, 2)
+        def _(r):
             rows = []
             for s in range(32):
                 src, j = s // 8, s % 8
-                total = got[src, e, j, r, pl.ds(d0, 16), :].astype(jnp.float32)
+                total = got[src, e, j, r].astype(jnp.float32)
                 if src and j < 7:
-                    total = total + got[src - 1, e, j + 8, r, pl.ds(d0, 16), :].astype(jnp.float32)
+                    total = total + got[src - 1, e, j + 8, r].astype(jnp.float32)
                 rows.append(total)
             lined = jnp.swapaxes(jnp.stack(rows), 0, 1)
-            own[e, pl.ds(d0, 16), pl.ds(pl.multiple_of(r * 32, 32), 32), :] = lined.astype(jnp.bfloat16)
+            own[e, :, pl.ds(pl.multiple_of(r * 32, 32), 32), :] = lined.astype(jnp.bfloat16)
 
         pair(e, 0).start()
         pair(e, 1).start()
@@ -245,13 +248,10 @@
         first(e).start()
         mine(e).start()
     join_twins(0)
-    join_twins(1)
-    join_all(0)
-    join_twins(2)
-    join_all(1)
-    join_twins(3)
-    join_all(2)
-    join_all(3)
+    for e in range(1, SUBS):
+        join_twins(e)
+        join_all(e - 1)
+    join_all(SUBS - 1)
     pair(SUBS - 1, 0).wait_recv()
     pair(SUBS - 1, 2).start()
     for e in range(SUBS):
@@ -268,14 +268,13 @@
     del me_ref
     for e in range(4):
         for d in range(2):
-            own = own_ref[0, e, d]
-            both = jnp.concatenate([jnp.concatenate([own[:32], own[32:]], axis=0),
-                                    jnp.concatenate([own[32:], -own[:32]], axis=0)], axis=1)
-            every = jnp.concatenate([all_ref[i, e, d] for i in range(4)], axis=1)
-            res = lax.dot_general(both, every, (((0,), (0,)), ((), ())), preferred_element_type=jnp.float32)
-            res = (res * (1.0 / 32.0)).astype(jnp.bfloat16)
-            o_ref[0, 4 * d + e] = res[:128]
-            o_ref[1, 4 * d + e] = res[128:]
+            own = own_ref[0, e, d] * jnp.bfloat16(1.0 / 32.0)
+            turned = jnp.concatenate([own[32:], -own[:32]], axis=0)
+            for n in range(2):
+                every = jnp.concatenate([all_ref[2 * n, e, d], all_ref[2 * n + 1, e, d]], axis=1)
+                for part, left in enumerate((own, turned)):
+                    res = lax.dot_general(left, every, (((0,), (0,)), ((), ())), preferred_element_type=jnp.float32)
+                    o_ref[part, 4 * d + e, :, n * 256:(n + 1) * 256] = res.astype(jnp.bfloat16)
 
 
 def fast(voltages, scales):
@@ -283,24 +282,25 @@
     gains = (scales.astype(jnp.float32) * (1.0 / 256.0))[:, None]
     whole = lambda *shape: pl.BlockSpec(shape, lambda p: (0,) * len(shape))
     parts = pl.pallas_call(
-        front_kernel, grid=(6,),
-        out_shape=jax.ShapeDtypeStruct((2, 4, 4, 12, 2, 32, 128), jnp.bfloat16),
-        in_specs=[whole(128, 16384), whole(128, 1), whole(16, 1, NFFT), whole(2, 512, 1024), whole(2, 512, 2048)],
-        out_specs=pl.BlockSpec((2, 4, 4, 2, 2, 32, 128), lambda p: (0, 0, 0, p, 0, 0, 0)),
-        scratch_shapes=[pltpu.VMEM((256, NFFT), jnp.bfloat16)],
+        front_kernel, grid=(7,),
+        out_shape=jax.ShapeDtypeStruct((2, SUBS, 4, 12, 2, 16, 128), jnp.bfloat16),
+        in_specs=[whole(128, 16384), whole(128, 1), whole(18, 1, NFFT), whole(2, 512, 1024), whole(2, 512, 2048)],
+        out_specs=pl.BlockSpec((2, SUBS, 4, 2, 2, 16, 128), lambda p: (0, 0, 0, jnp.maximum(p - 1, 0), 0, 0, 0)),
+        scratch_shapes=[pltpu.VMEM((128, 4 * NFFT), jnp.float32), pltpu.VMEM((256, NFFT), jnp.bfloat16),
+                        pltpu.VMEM((256, NFFT), jnp.bfloat16)],
         compiler_params=pltpu.CompilerParams(vmem_limit_bytes=56 << 20),
         name="filter_transform",
     )(voltages, gains, wide[:, None], even, odd)
     gathered = pl.pallas_call(
         comm_kernel,
-        out_shape=jax.ShapeDtypeStruct((4, SUBS, 32, 64, 128), jnp.bfloat16),
+        out_shape=jax.ShapeDtypeStruct((4, SUBS, 16, 64, 128), jnp.bfloat16),
         in_specs=[pl.BlockSpec(memory_space=pl.ANY)],
         out_specs=pl.BlockSpec(memory_space=pl.ANY),
         scratch_shapes=[
-            pltpu.VMEM((2, SUBS, 4, PART, 2, 32, 128), jnp.bfloat16),
-            pltpu.VMEM((SUBS, 4, PART + 4, 2, 32, 128), jnp.bfloat16),
-            pltpu.VMEM((4, SUBS, PART + 4, 2, 32, 128), jnp.bfloat16),
-            pltpu.VMEM((SUBS, 32, 64, 128), jnp.bfloat16),
+            pltpu.VMEM((2, SUBS, 4, PART, 2, 16, 128), jnp.bfloat16),
+            pltpu.VMEM((SUBS, 4, PART + 4, 2, 16, 128), jnp.bfloat16),
+            pltpu.VMEM((4, SUBS, PART + 4, 2, 16, 128), jnp.bfloat16),
+            pltpu.VMEM((SUBS, 16, 64, 128), jnp.bfloat16),
             pltpu.SemaphoreType.DMA((SUBS,)), pltpu.SemaphoreType.DMA((SUBS,)),
             pltpu.SemaphoreType.DMA((SUBS, 4)), pltpu.SemaphoreType.DMA((SUBS, 4)),
             pltpu.SemaphoreType.DMA((SUBS, 3)),
@@ -309,7 +309,7 @@
         compiler_params=pltpu.CompilerParams(
             collective_id=0, has_side_effects=True, vmem_limit_bytes=48 << 20),
         name="turn_and_share",
-    )(parts)
+    )(parts).reshape(4, 4, 32, 64, 128)
     me = lax.axis_index("inp").astype(jnp.int32).reshape(1)
     return pl.pallas_call(
         pair_kernel,

time: 175 us -> 161 us (0.920)
  Pallas kernels: 173 us -> 159 us
    pallas_call x2, Pallas kernels: 151 us -> 138 us  [the longest x1 108 us: fast(): pl.pallas_call(comm_kernel, out_shape=jax.ShapeDtypeStruct((4, SUBS, 16,...]
where the time goes in v3:
time: 161 us
  Pallas kernels  159 us (99%)
    pallas_call x1, Pallas kernels, fast(): pl.pallas_call(comm_kernel, out_shape=jax.ShapeDtypeStruct((4, SUBS, 16,...  108 us
    pallas_call x1, Pallas kernels, fast(): pl.pallas_call(front_kernel, grid=(7,), out_shape=jax.ShapeDtypeStruct((2...  29.7 us
    pallas_call x1, Pallas kernels, fast(): pl.pallas_call(pair_kernel, out_shape=jax.ShapeDtypeStruct((2, 128, 128,...  21.1 us

profile of v3, /device:TPU:17, one launch (start us, length us, event | category | flops | bytes accessed | tf_op | source)
XLA Modules:
  0.0 160.6 jit_solution(8541539950168966344)
XLA Ops:
  0.0 0.7 multiply_bitcast_fusion
  0.7 0.7 copy.6.g_ref
  1.4 29.7 %filter_transform.1.p_ref = bf16[2,8,4,12,2,16,128]{6,5,4,3,2,1,0:T(8,128)(2,1)} custom-call(s32[128,16384]{1,0:T(8,128)} %x_ref.1, f32[128,1]{1,0:T(8,128)} %copy.6.g_ref, f32[18,1,4096]{2,1,0:T(1,128)} %constant.15.w_ref, bf16[2,512,1024]{2,1,0:T(8,128)(2,1)} %constant.13.clone.even_ref, bf16[2,512,2048]{2,1,0:T(8,128)(2,1)} %constant.14.clone.odd_ref), custom_call_target="tpu_custom_call" | custom-call | tf_op jit(solution)/shard_map/filter_transform/pallas_call | solution.py:284
  31.1 108.4 %turn_and_share.1 = bf16[4,8,16,64,128]{4,3,2,1,0:T(8,128)(2,1)} custom-call(bf16[2,8,4,12,2,16,128]{6,5,4,3,2,1,0:T(8,128)(2,1)} %filter_transform.1.p_ref), custom_call_target="tpu_custom_call" | custom-call | tf_op jit(solution)/shard_map/turn_and_share/pallas_call | solution.py:294
  139.5 21.1 %correlate.1 = bf16[2,128,128,512]{3,2,1,0:T(8,128)(2,1)} custom-call(s32[1]{0:T(128)} %bitcast.me_ref, bf16[4,4,32,64,128]{4,3,2,1,0:T(8,128)(2,1)} %bitcast.4, bf16[4,4,32,64,128]{4,3,2,1,0:T(8,128)(2,1)} %bitcast.5), custom_call_target="tpu_custom_call" | custom-call | tf_op jit(solution)/shard_map/correlate/pallas_call | solution.py:314

commit v4 on v3

--- a/solution.py
+++ b/solution.py
@@ -156,7 +156,7 @@
     y_ref[...] = new_ref[...]
 
 
-def comm_kernel(p_ref, o_ref, near, comb, got, own, ysend, yrecv, zsend, zrecv, loc_sem, xsend, xrecv):
+def comm_kernel(p_ref, o_ref, near, comb, got, own, passed, ysend, yrecv, zsend, zrecv, loc_sem, xsend, xrecv, rsend, rrecv):
     me = lax.axis_index("chan")
     inp = lax.axis_index("inp")
     z, y = me // 2, lax.rem(me, 2)
@@ -183,11 +183,28 @@
     def mine(e):
         return pltpu.make_async_copy(p_ref.at[y, e, :, pl.ds(0, PART)], near.at[y, e], loc_sem.at[e, 0])
 
-    def turn(e, k):
+    def turn(e, k, count):
         return pltpu.make_async_remote_copy(
-            src_ref=comb.at[e, far(k)], dst_ref=got.at[z, e],
+            src_ref=comb.at[e, far(k), pl.ds(0, count)], dst_ref=got.at[z, e, pl.ds(0, count)],
             send_sem=zsend.at[e, k], recv_sem=zrecv.at[e, k],
             device_id={"chan": 2 * far(k) + y}, device_id_type=MESH)
+
+    def either(source, target, act):
+        short = (source == 3) | ((source == 0) & (target >= 2))
+
+        @pl.when(short)
+        def _():
+            act(8)
+
+        @pl.when(jnp.logical_not(short))
+        def _():
+            act(PART + 4)
+
+    def relay(e):
+        return pltpu.make_async_remote_copy(
+            src_ref=comb.at[e, pl.ds(2, 2), pl.ds(8, 7)], dst_ref=passed.at[e],
+            send_sem=rsend.at[e], recv_sem=rrecv.at[e],
+            device_id={"chan": lax.rem(me + 2, 8)}, device_id_type=MESH)
 
     def stay(e):
         return pltpu.make_async_copy(comb.at[e, z], got.at[z, e], loc_sem.at[e, 1])
@@ -216,14 +233,28 @@
                         total = term if total is None else total + term
                 comb[e, to, j] = total.astype(jnp.bfloat16)
 
+        @pl.when(z == 0)
+        def _():
+            relay(e).start()
+
+        @pl.when(z == 1)
+        def _():
+            relay(e).wait_recv()
+
+            @pl.loop(0, 2)
+            def _(i):
+                for j in range(7):
+                    total = comb[e, 2 + i, j].astype(jnp.float32) + passed[e, i, j].astype(jnp.float32)
+                    comb[e, 2 + i, j] = total.astype(jnp.bfloat16)
+
         for k in (2, 1, 3):
-            turn(e, k).start()
+            either(z, far(k), lambda count: turn(e, k, count).start())
         stay(e).start()
 
     def join_all(e):
         stay(e).wait()
         for k in range(1, 4):
-            turn(e, k).wait_recv()
+            either(far(4 - k), z, lambda count: turn(e, k, count).wait_recv())
 
         @pl.loop(0, 2)
         def _(r):
@@ -247,6 +278,11 @@
     for e in range(SUBS):
         first(e).start()
         mine(e).start()
+
+    @pl.when(z >= 2)
+    def _():
+        got[0, :, 8:] = jnp.zeros((SUBS, 7, 2, 16, 128), jnp.bfloat16)
+
     join_twins(0)
     for e in range(1, SUBS):
         join_twins(e)
@@ -254,10 +290,15 @@
     join_all(SUBS - 1)
     pair(SUBS - 1, 0).wait_recv()
     pair(SUBS - 1, 2).start()
+    @pl.when(z == 0)
+    def _():
+        for e in range(SUBS):
+            relay(e).wait_send()
+
     for e in range(SUBS):
         first(e).wait_send()
         for k in range(1, 4):
-            turn(e, k).wait_send()
+            either(z, far(k), lambda count: turn(e, k, count).wait_send())
         keep(e).wait()
         pair(e, 0).wait_send()
         pair(e, 1).wait()
@@ -301,10 +342,12 @@
             pltpu.VMEM((SUBS, 4, PART + 4, 2, 16, 128), jnp.bfloat16),
             pltpu.VMEM((4, SUBS, PART + 4, 2, 16, 128), jnp.bfloat16),
             pltpu.VMEM((SUBS, 16, 64, 128), jnp.bfloat16),
+            pltpu.VMEM((SUBS, 2, 7, 2, 16, 128), jnp.bfloat16),
             pltpu.SemaphoreType.DMA((SUBS,)), pltpu.SemaphoreType.DMA((SUBS,)),
             pltpu.SemaphoreType.DMA((SUBS, 4)), pltpu.SemaphoreType.DMA((SUBS, 4)),
             pltpu.SemaphoreType.DMA((SUBS, 3)),
             pltpu.SemaphoreType.DMA((SUBS, 3)), pltpu.SemaphoreType.DMA((SUBS, 3)),
+            pltpu.SemaphoreType.DMA((SUBS,)), pltpu.SemaphoreType.DMA((SUBS,)),
         ],
         compiler_params=pltpu.CompilerParams(
             collective_id=0, has_side_effects=True, vmem_limit_bytes=48 << 20),

time: 161 us -> 144 us (0.89)
  Pallas kernels: 159 us -> 142 us
    pallas_call x1, Pallas kernels: 108 us -> 91.6 us  [fast(): pl.pallas_call(comm_kernel, out_shape=jax.ShapeDtypeStruct((4, SUBS, 16,...]
where the time goes in v4:
time: 144 us
  Pallas kernels  142 us (99%)
    pallas_call x1, Pallas kernels, fast(): pl.pallas_call(comm_kernel, out_shape=jax.ShapeDtypeStruct((4, SUBS, 16,...  91.6 us
    pallas_call x1, Pallas kernels, fast(): pl.pallas_call(front_kernel, grid=(7,), out_shape=jax.ShapeDtypeStruct((2...  29.7 us
    pallas_call x1, Pallas kernels, fast(): pl.pallas_call(pair_kernel, out_shape=jax.ShapeDtypeStruct((2, 128, 128,...  21.1 us

profile of v4, /device:TPU:17, one launch (start us, length us, event | category | flops | bytes accessed | tf_op | source)
XLA Modules:
  0.0 143.8 jit_solution(2675751039874479494)
XLA Ops:
  0.0 0.7 multiply_bitcast_fusion
  0.7 0.7 copy.6.g_ref
  1.4 29.7 %filter_transform.1.p_ref = bf16[2,8,4,12,2,16,128]{6,5,4,3,2,1,0:T(8,128)(2,1)} custom-call(s32[128,16384]{1,0:T(8,128)} %x_ref.1, f32[128,1]{1,0:T(8,128)} %copy.6.g_ref, f32[18,1,4096]{2,1,0:T(1,128)} %constant.15.w_ref, bf16[2,512,1024]{2,1,0:T(8,128)(2,1)} %constant.13.clone.even_ref, bf16[2,512,2048]{2,1,0:T(8,128)(2,1)} %constant.14.clone.odd_ref), custom_call_target="tpu_custom_call" | custom-call | tf_op jit(solution)/shard_map/filter_transform/pallas_call | solution.py:325
  31.1 91.6 %turn_and_share.1 = bf16[4,8,16,64,128]{4,3,2,1,0:T(8,128)(2,1)} custom-call(bf16[2,8,4,12,2,16,128]{6,5,4,3,2,1,0:T(8,128)(2,1)} %filter_transform.1.p_ref), custom_call_target="tpu_custom_call" | custom-call | tf_op jit(solution)/shard_map/turn_and_share/pallas_call | solution.py:335
  122.7 21.1 %correlate.1 = bf16[2,128,128,512]{3,2,1,0:T(8,128)(2,1)} custom-call(s32[1]{0:T(128)} %bitcast.me_ref, bf16[4,4,32,64,128]{4,3,2,1,0:T(8,128)(2,1)} %bitcast.4, bf16[4,4,32,64,128]{4,3,2,1,0:T(8,128)(2,1)} %bitcast.5), custom_call_target="tpu_custom_call" | custom-call | tf_op jit(solution)/shard_map/correlate/pallas_call | solution.py:357

commit v5 on v4

--- a/solution.py
+++ b/solution.py
@@ -110,7 +110,7 @@
     return wide, np.stack([out[0], out[2]]), np.stack([out[1], out[3]])
 
 
-def front_kernel(x_ref, g_ref, w_ref, even_ref, odd_ref, o_ref, f_ref, new_ref, y_ref):
+def front_kernel(x_ref, g_ref, w_ref, even_ref, odd_ref, o_ref, f_ref, y_ref):
     p = pl.program_id(0)
     rows, span, quarter = 32, 256, NFFT // 4
     nt = (((1,), (1,)), ((), ()))
@@ -136,11 +136,12 @@
             a, b2 = f[0] + f[2], f[1] + f[3]
             at = half * 128 + r0
             for j, v in enumerate((a + b2, a - b2, f[0] - f[2], f[1] - f[3])):
-                new_ref[at:at + rows, j * quarter + l * span:j * quarter + (l + 1) * span] = v.astype(jnp.bfloat16)
-
+                y_ref[at:at + rows, j * quarter + l * span:j * quarter + (l + 1) * span] = v.astype(jnp.bfloat16)
+
+    for chunk in range(4):
+        filter_rows(0, chunk * rows)
+        filter_rows(1, chunk * rows)
     for e in range(4):
-        filter_rows(0, e * rows)
-        filter_rows(1, e * rows)
         for part in range(2):
             sel = pl.ds(part * 256, 256)
             if e % 2 == 0:
@@ -153,7 +154,6 @@
                 for y_to in range(2):
                     for d in range(2):
                         o_ref[y_to, 2 * e + d, 2 * part:2 * part + 2, half] = blocks[:, y_to, :, d]
-    y_ref[...] = new_ref[...]
 
 
 def comm_kernel(p_ref, o_ref, near, comb, got, own, passed, ysend, yrecv, zsend, zrecv, loc_sem, xsend, xrecv, rsend, rrecv):
@@ -305,11 +305,11 @@
         pair(e, 2).wait()
 
 
-def pair_kernel(me_ref, all_ref, own_ref, o_ref):
-    del me_ref
+def pair_kernel(me_ref, all_ref, o_ref):
+    me = me_ref[0]
     for e in range(4):
-        for d in range(2):
-            own = own_ref[0, e, d] * jnp.bfloat16(1.0 / 32.0)
+        for d in range(4):
+            own = all_ref[me, e, d] * jnp.bfloat16(1.0 / 32.0)
             turned = jnp.concatenate([own[32:], -own[:32]], axis=0)
             for n in range(2):
                 every = jnp.concatenate([all_ref[2 * n, e, d], all_ref[2 * n + 1, e, d]], axis=1)
@@ -323,12 +323,11 @@
     gains = (scales.astype(jnp.float32) * (1.0 / 256.0))[:, None]
     whole = lambda *shape: pl.BlockSpec(shape, lambda p: (0,) * len(shape))
     parts = pl.pallas_call(
-        front_kernel, grid=(7,),
+        front_kernel, grid=(6,),
         out_shape=jax.ShapeDtypeStruct((2, SUBS, 4, 12, 2, 16, 128), jnp.bfloat16),
         in_specs=[whole(128, 16384), whole(128, 1), whole(18, 1, NFFT), whole(2, 512, 1024), whole(2, 512, 2048)],
-        out_specs=pl.BlockSpec((2, SUBS, 4, 2, 2, 16, 128), lambda p: (0, 0, 0, jnp.maximum(p - 1, 0), 0, 0, 0)),
-        scratch_shapes=[pltpu.VMEM((128, 4 * NFFT), jnp.float32), pltpu.VMEM((256, NFFT), jnp.bfloat16),
-                        pltpu.VMEM((256, NFFT), jnp.bfloat16)],
+        out_specs=pl.BlockSpec((2, SUBS, 4, 2, 2, 16, 128), lambda p: (0, 0, 0, p, 0, 0, 0)),
+        scratch_shapes=[pltpu.VMEM((128, 4 * NFFT), jnp.float32), pltpu.VMEM((256, NFFT), jnp.bfloat16)],
         compiler_params=pltpu.CompilerParams(vmem_limit_bytes=56 << 20),
         name="filter_transform",
     )(voltages, gains, wide[:, None], even, odd)
@@ -358,13 +357,12 @@
         pair_kernel,
         out_shape=jax.ShapeDtypeStruct((2, 128, 128, 512), jnp.bfloat16),
         grid_spec=pltpu.PrefetchScalarGridSpec(
-            num_scalar_prefetch=1, grid=(16,),
-            in_specs=[pl.BlockSpec((4, 4, 2, 64, 128), lambda g, m: (0, 0, g, 0, 0)),
-                      pl.BlockSpec((1, 4, 2, 64, 128), lambda g, m: (m[0], 0, g, 0, 0))],
-            out_specs=pl.BlockSpec((2, 8, 128, 512), lambda g, m: (0, g, 0, 0))),
+            num_scalar_prefetch=1, grid=(8,),
+            in_specs=[pl.BlockSpec((4, 4, 4, 64, 128), lambda g, m: (0, 0, g, 0, 0))],
+            out_specs=pl.BlockSpec((2, 16, 128, 512), lambda g, m: (0, g, 0, 0))),
         compiler_params=pltpu.CompilerParams(vmem_limit_bytes=48 << 20),
         name="correlate",
-    )(me, gathered, gathered)
+    )(me, gathered)
 
 
 def solution(mesh):

time: 144 us -> 138 us (0.958)
  Pallas kernels: 142 us -> 137 us
    pallas_call x1, Pallas kernels: 21.1 us -> 16.7 us  [fast(): pl.pallas_call(pair_kernel, out_shape=jax.ShapeDtypeStruct((2, 128, 128,...]
    pallas_call x1, Pallas kernels: 29.7 us -> 28.3 us  [fast(): pl.pallas_call(front_kernel, grid=(6,), out_shape=jax.ShapeDtypeStruct((2...]
where the time goes in v5:
time: 138 us
  Pallas kernels  137 us (99%)
    pallas_call x1, Pallas kernels, fast(): pl.pallas_call(comm_kernel, out_shape=jax.ShapeDtypeStruct((4, SUBS, 16,...  91.6 us
    pallas_call x1, Pallas kernels, fast(): pl.pallas_call(front_kernel, grid=(6,), out_shape=jax.ShapeDtypeStruct((2...  28.3 us
    pallas_call x1, Pallas kernels, fast(): pl.pallas_call(pair_kernel, out_shape=jax.ShapeDtypeStruct((2, 128, 128,...  16.7 us

profile of v5, /device:TPU:17, one launch (start us, length us, event | category | flops | bytes accessed | tf_op | source)
XLA Modules:
  0.0 137.9 jit_solution(11996035788510299922)
XLA Ops:
  0.0 0.7 multiply_bitcast_fusion
  0.7 0.7 copy.6.g_ref
  1.4 28.3 %filter_transform.1.p_ref = bf16[2,8,4,12,2,16,128]{6,5,4,3,2,1,0:T(8,128)(2,1)} custom-call(s32[128,16384]{1,0:T(8,128)} %x_ref.1, f32[128,1]{1,0:T(8,128)} %copy.6.g_ref, f32[18,1,4096]{2,1,0:T(1,128)} %constant.15.w_ref, bf16[2,512,1024]{2,1,0:T(8,128)(2,1)} %constant.13.clone.even_ref, bf16[2,512,2048]{2,1,0:T(8,128)(2,1)} %constant.14.clone.odd_ref), custom_call_target="tpu_custom_call" | custom-call | tf_op jit(solution)/shard_map/filter_transform/pallas_call | solution.py:325
  29.6 91.6 %turn_and_share.1 = bf16[4,8,16,64,128]{4,3,2,1,0:T(8,128)(2,1)} custom-call(bf16[2,8,4,12,2,16,128]{6,5,4,3,2,1,0:T(8,128)(2,1)} %filter_transform.1.p_ref), custom_call_target="tpu_custom_call" | custom-call | tf_op jit(solution)/shard_map/turn_and_share/pallas_call | solution.py:334
  121.3 16.7 %correlate.1 = bf16[2,128,128,512]{3,2,1,0:T(8,128)(2,1)} custom-call(s32[1]{0:T(128)} %bitcast.me_ref, bf16[4,4,32,64,128]{4,3,2,1,0:T(8,128)(2,1)} %bitcast.4), custom_call_target="tpu_custom_call" | custom-call | tf_op jit(solution)/shard_map/correlate/pallas_call | solution.py:356
